TPU v7x, 32 devices: a whole 2x2x4 slice. The times are simulated.
32 devices in a mesh: dp: 16 (over z, y, core), mp: 2 (over x).
Axes of the slice: x: 2, y: 2, z: 4, core: 2. Of those that a mesh axis runs over, the one named last changes fastest.
Arguments:
- activations: bfloat16 [2, 32, 384, 14336], P(None, 'dp', None, 'mp'), may hold values from -6 to 6
- out_grads: bfloat16 [2, 32, 384, 4096], P(None, 'dp', None, 'mp'), may hold values from -6 to 6
- proj_in: bfloat16 [14336, 64], P('mp'), may hold values from -0.046875 to 0.046875
- proj_out: bfloat16 [4096, 64], P('mp'), may hold values from -0.09375 to 0.09375
- store: bfloat16 [2, 8192, 4096], P(None, ('dp', 'mp')), may hold values from -0.09375 to 0.09375
- ckpt_rate: float32 [2], replicated, may hold values from 0.5 to 2
- store_group: int32 [8192], P(('dp', 'mp')), may hold values from 0 to 15
Outputs:
- scores: float32 [32, 8192], P(None, ('dp', 'mp'))
- group_scores: float32 [32, 16], replicated
All inputs are finite; a program needn't handle non-finite values.
Results may differ from a plain program's by a relative error of at most 0.005.
Values may be sent and summed in bfloat16 or wider, within the bound.
A program may use at most 64 MiB of HBM per device.

v0:
```python
import jax
import jax.numpy as jnp
from jax import lax
from jax.sharding import PartitionSpec as P

GROUPS = 16


def shards(activations, out_grads, proj_in, proj_out, store, ckpt_rate, store_group):
    rank = proj_in.shape[1]
    seq_len = activations.shape[2]
    ex_local = activations.shape[1]
    scale = 1.0 / jnp.sqrt(jnp.float32(seq_len))
    part_in = jnp.einsum("cesf,fr->cesr", activations, proj_in, preferred_element_type=jnp.float32)
    part_out = jnp.einsum("cesf,fr->cesr", out_grads, proj_out, preferred_element_type=jnp.float32)
    stacked = jnp.concatenate([part_in, part_out], axis=3)
    summed = lax.psum(stacked, "mp")
    low_in = summed[..., :rank].astype(jnp.bfloat16)
    low_grad = summed[..., rank:].astype(jnp.bfloat16)
    outer = jnp.einsum("cesa,cesb->ecab", low_in, low_grad, preferred_element_type=jnp.float32)
    query = (outer.reshape(ex_local, 2, rank * rank) * scale).astype(jnp.bfloat16)
    piece = lax.all_gather(query, "dp", axis=0, tiled=True)
    first = jnp.einsum("qk,rk->qr", piece[:, 0], store[0], preferred_element_type=jnp.float32)
    second = jnp.einsum("qk,rk->qr", piece[:, 1], store[1], preferred_element_type=jnp.float32)
    scores = ckpt_rate[0] * first + ckpt_rate[1] * second
    member = (store_group[:, None] == jnp.arange(GROUPS, dtype=jnp.int32)[None, :]).astype(
        jnp.float32
    )
    partial_totals = jnp.dot(scores, member, precision=lax.Precision.HIGHEST)
    totals = lax.psum(partial_totals, ("dp", "mp"))
    store_rows = store.shape[1] * lax.axis_size("dp") * lax.axis_size("mp")
    group_scores = totals / jnp.sqrt(jnp.float32(store_rows) / jnp.float32(GROUPS))
    return (scores, group_scores)


def solution(mesh):
    placed = (
        P(None, "dp", None, "mp"),
        P(None, "dp", None, "mp"),
        P("mp", None),
        P("mp", None),
        P(None, ("dp", "mp"), None),
        P(),
        P(("dp", "mp")),
    )
    return jax.shard_map(
        shards, mesh=mesh, in_specs=placed, out_specs=(P(None, ("dp", "mp")), P()), check_vma=False
    )
```

profile of v0, /device:TPU:0, one launch (start us, length us, event | category | flops | bytes accessed | tf_op | source)
XLA Modules:
  0.0 107.7 jit_solution(17200616766764767566)
XLA Ops:
  0.6 0.0 copy-start
  0.6 0.0 copy-start.2
  0.7 0.0 copy-start.1
  0.7 1.1 %copy-done = bf16[7168,64]{0,1:T(8,128)(2,1)S(1)} copy-done((bf16[7168,64]{0,1:T(8,128)(2,1)S(1)}, bf16[7168,64]{0,1:T(8,128)(2,1)}, u32[]{:S(2)}) %copy-start) | copy-done | bytes 917528
  1.8 11.5 %fusion.16 = f32[2,2,384,64]{2,3,1,0:T(8,128)S(1)} fusion(bf16[2,2,384,7168]{3,2,1,0:T(8,128)(2,1)} %param.7, bf16[7168,64]{0,1:T(8,128)(2,1)S(1)} %copy-done), kind=kOutput, calls=%fused_computation.11 | convolution fusion | flops 1409286144 | bytes 23330816 | tf_op jit(solution)/shard_map/cesf,fr->cesr/dot_general | solution.py:14
  13.3 0.0 copy-done.2
  13.4 0.0 copy-done.1
  13.4 2.0 %fusion.18 = f32[2,2,384,64]{2,3,1,0:T(8,128)S(1)} fusion(bf16[2,2,384,2048]{3,2,1,0:T(8,128)(2,1)S(1)} %copy-done.1, bf16[2048,64]{0,1:T(8,128)(2,1)S(1)} %copy-done.2), kind=kOutput, calls=%fused_computation.16 | convolution fusion | flops 402653184 | bytes 6946816 | tf_op jit(solution)/shard_map/cesf,fr->cesr/dot_general | solution.py:15
  15.4 0.0 copy-start.3
  15.4 0.1 pad_maximum_fusion
  15.5 24.5 %all-reduce.1 = bf16[2,2,384,128]{2,3,1,0:T(8,128)(2,1)S(1)} all-reduce(f32[2,2,384,128]{2,3,1,0:T(8,128)S(1)} %pad_maximum_fusion), channel_id=1, replica_groups=mesh['dp'=16,'mp'=2] {'mp'}, use_global_device_ids=true, to_apply=%region_0.0 | all-reduce | flops 196608 | bytes 1179648 | tf_op jit(solution)/shard_map/psum | solution.py:17
  40.0 0.0 copy-start.5
  40.0 0.2 fusion.6
  40.2 0.1 convert_element_type.10
  40.4 0.0 copy-start.4
  40.4 23.4 %all_gather.3 = bf16[32,2,4096]{2,1,0:T(2,128)(2,1)S(1)} all-gather(bf16[2,2,4096]{2,1,0:T(2,128)(2,1)S(1)} %convert_element_type.10), channel_id=1, replica_groups=mesh['dp'=16,'mp'=2] {'dp'}, dimensions={0}, use_global_device_ids=true | all-gather | bytes 557056 | tf_op jit(solution)/shard_map/all_gather | solution.py:22
  63.8 1.2 %fusion.24 = (bf16[32,1,4096]{2,1,0:T(2,128)(2,1)S(1)}, bf16[32,1,4096]{2,1,0:T(2,128)(2,1)S(1)}) fusion(bf16[32,2,4096]{2,1,0:T(2,128)(2,1)S(1)} %all_gather.3), kind=kLoop, calls=%fused_computation.24 | loop fusion | bytes 1048576 | tf_op jit(solution)/shard_map/slice | solution.py:23
  65.0 0.0 copy-done.3
  65.0 0.6 fusion.26
  65.6 2.9 %fusion.13 = f32[32,256]{1,0:T(8,128)S(1)} fusion(bf16[2,256,4096]{2,1,0:T(8,128)(2,1)} %param.11, bf16[32,1,4096]{2,1,0:T(2,128)(2,1)S(1)} %get-tuple-element.3, f32[]{:T(128)} %bitcast.7), kind=kOutput, calls=%fused_computation.10 | convolution fusion | flops 67117056 | bytes 2392576 | tf_op jit(solution)/shard_map/qk,rk->qr/dot_general | solution.py:24
  68.5 0.0 copy-done.4
  68.5 1.3 %fusion.10 = f32[32,256]{1,0:T(8,128)S(1)} fusion(f32[32,256]{1,0:T(8,128)S(1)} %fusion.13, bf16[2,256,4096]{2,1,0:T(8,128)(2,1)S(1)} %copy-done.4, bf16[32,1,4096]{2,1,0:T(2,128)(2,1)S(1)} %get-tuple-element.2, f32[]{:T(128)} %bitcast), kind=kOutput, calls=%fused_computation.9 | convolution fusion | flops 67125248 | bytes 2686980 | tf_op jit(solution)/shard_map/qk,rk->qr/dot_general | solution.py:23
  69.9 0.0 copy-done.5
  69.9 0.0 copy-start.6
  69.9 0.3 fusion.22
  70.2 36.9 %psum.15 = f32[32,16]{0,1:T(8,128)S(1)} all-reduce(f32[32,16]{0,1:T(8,128)S(1)} %fusion.22), channel_id=1, replica_groups=mesh['dp'=16,'mp'=2] {'dp','mp'}, use_global_device_ids=true, to_apply=%region_1.0 | all-reduce | flops 512 | bytes 4096 | tf_op jit(solution)/shard_map/psum | solution.py:30
  107.1 0.6 broadcast_multiply_fusion
  107.7 0.0 copy-done.6
  (1 shorter events, 0.0 us)
Async XLA Ops:
  0.6 1.2 %copy-start = (bf16[7168,64]{0,1:T(8,128)(2,1)S(1)}, bf16[7168,64]{0,1:T(8,128)(2,1)}, u32[]{:S(2)}) copy-start(bf16[7168,64]{0,1:T(8,128)(2,1)} %param.9) | copy-start | bytes 2752516
  0.6 12.7 %copy-start.2 = (bf16[2048,64]{0,1:T(8,128)(2,1)S(1)}, bf16[2048,64]{0,1:T(8,128)(2,1)}, u32[]{:S(2)}) copy-start(bf16[2048,64]{0,1:T(8,128)(2,1)} %param.10) | copy-start | bytes 786436
  0.7 12.7 %copy-start.1 = (bf16[2,2,384,2048]{3,2,1,0:T(8,128)(2,1)S(1)}, bf16[2,2,384,2048]{3,2,1,0:T(8,128)(2,1)}, u32[]{:S(2)}) copy-start(bf16[2,2,384,2048]{3,2,1,0:T(8,128)(2,1)} %param.8) | copy-start | bytes 18874372
  15.4 49.6 %copy-start.3 = (f32[2]{0:T(128)S(1)}, f32[2]{0:T(128)}, u32[]{:S(2)}) copy-start(f32[2]{0:T(128)} %param.12) | copy-start | bytes 28
  40.0 29.9 %copy-start.5 = (s32[256]{0:T(256)S(1)}, s32[256]{0:T(256)}, u32[]{:S(2)}) copy-start(s32[256]{0:T(256)} %param.13) | copy-start | bytes 3076
  40.4 28.2 %copy-start.4 = (bf16[2,256,4096]{2,1,0:T(8,128)(2,1)S(1)}, bf16[2,256,4096]{2,1,0:T(8,128)(2,1)}, u32[]{:S(2)}) copy-start(bf16[2,256,4096]{2,1,0:T(8,128)(2,1)} %param.11) | copy-start | bytes 12582916
  69.9 37.8 %copy-start.6 = (f32[32,256]{1,0:T(8,128)}, f32[32,256]{1,0:T(8,128)S(1)}, u32[]{:S(2)}) copy-start(f32[32,256]{1,0:T(8,128)S(1)} %fusion.10) | copy-start | bytes 98308
where the time goes:
time: 109 us; the launch traced here: 108 us
  blocking collectives  84.8 us (78%)
  matrix products  18.3 us (17%)
  local copies, waits for them, and re-layouts  3.12 us (3%)
    psum x1, blocking collectives, shards(): totals = lax.psum(partial_totals, ('dp', 'mp'))  36.9 us
    psum x1, blocking collectives, shards(): summed = lax.psum(stacked, 'mp')  24.5 us
    all_gather x1, blocking collectives, shards(): piece = lax.all_gather(query, 'dp', axis=0, tiled=True)  23.4 us
    dot_general x1, matrix products, shards(): jnp.einsum('cesf,fr->cesr', activations, proj_in, preferred_element_type=...  11.5 us
    dot_general x1, matrix products, shards(): jnp.einsum('qk,rk->qr', piece[:, 1], store[1], preferred_element_type=jnp...  2.95 us

commit v1 on v0

--- a/solution.py
+++ b/solution.py
@@ -1,9 +1,282 @@
+import functools
 import jax
 import jax.numpy as jnp
 from jax import lax
+from jax.experimental import pallas as pl
+from jax.experimental.pallas import tpu as pltpu
 from jax.sharding import PartitionSpec as P
 
 GROUPS = 16
+MESH = pl.DeviceIdType.MESH
+NZ = 4
+HALVES = 2
+CUBE = ((1, 0, 0), (0, 1, 0), (1, 1, 0), (0, 0, 1), (1, 0, 1), (0, 1, 1), (1, 1, 1))
+PLANE = ((1, 0), (0, 1), (1, 1))
+
+
+def nt_dot(a, b, **kw):
+    return lax.dot_general(
+        a, b, (((1,), (1,)), ((), ())), preferred_element_type=jnp.float32, **kw
+    )
+
+
+def kernel(
+    norm, scale,
+    act, grad, pin, pout, store, rate, group,
+    scores_o, group_o,
+    abuf, gbuf, wi, wo, sbuf, part, sendb, recvb, piece, wide, q, tmp, t1, t2,
+    load_sem, w_sem, store_sem, xs, xr, zs, zr, ps, pr, cs, cr, as_, ar, bs, br,
+):
+    dp = lax.axis_index("dp")
+    x = lax.axis_index("mp")
+    z = dp // 4
+    y = (dp // 2) % 2
+    c = dp % 2
+    rank = pin.shape[0]
+    ff = act.shape[3]
+    cols = ff // HALVES
+
+    def flip(v, on):
+        return 1 - v if on else v
+
+    def where_is(z_, y_, c_, x_):
+        return ((z_ * 2 + y_) * 2 + c_, x_)
+
+    def loads(p):
+        ck = (1 - x) + (p // 2) * (2 * x - 1)
+        e = p % 2
+        out = [pltpu.make_async_copy(grad.at[ck, e], gbuf.at[p], load_sem.at[p, 0])]
+        for h in range(HALVES):
+            span = pl.ds(h * cols, cols)
+            out.append(
+                pltpu.make_async_copy(
+                    act.at[ck, e, :, span], abuf.at[p, :, span], load_sem.at[p, 1 + h]
+                )
+            )
+        return out
+
+    w_in = pltpu.make_async_copy(pin, wi.at[pl.ds(0, rank)], w_sem.at[0])
+    w_out = pltpu.make_async_copy(pout, wo.at[pl.ds(rank, rank)], w_sem.at[1])
+    get_store = pltpu.make_async_copy(store, sbuf, store_sem)
+
+    w_out.start()
+    first = loads(0)
+    first[0].start()
+    w_in.start()
+    for copy in first[1:]:
+        copy.start()
+
+    barrier = pltpu.get_barrier_semaphore()
+    friends = [where_is((z + j) % NZ, y, c, x) for j in range(1, NZ)]
+    friends += [where_is(z, flip(y, dy), flip(c, dc), flip(x, dx)) for dx, dy, dc in CUBE]
+    for friend in friends:
+        pl.semaphore_signal(barrier, inc=1, device_id=friend, device_id_type=MESH)
+
+    wi[pl.ds(rank, rank), :] = jnp.zeros((rank, ff), wi.dtype)
+    wo[pl.ds(0, rank), :] = jnp.zeros((rank, wo.shape[1]), wo.dtype)
+    pl.semaphore_wait(barrier, len(friends))
+    w_out.wait()
+    w_in.wait()
+
+    def partial_copy(p):
+        return pltpu.make_async_remote_copy(
+            sendb.at[p], recvb.at[p], xs.at[p], xr.at[p],
+            device_id=where_is(z, y, c, 1 - x), device_id_type=MESH,
+        )
+
+    @pl.loop(0, 4)
+    def _(p):
+        @pl.when(p < 3)
+        def _():
+            for copy in loads(p + 1):
+                copy.start()
+
+        @pl.when(p == 3)
+        def _():
+            get_store.start()
+
+        here = loads(p)
+        here[0].wait()
+        acc = nt_dot(gbuf[p], wo[...])
+        for h in range(HALVES):
+            here[1 + h].wait()
+            acc += nt_dot(abuf[p, :, h * cols : (h + 1) * cols], wi[:, h * cols : (h + 1) * cols])
+
+        @pl.when(p < 2)
+        def _():
+            sendb[p] = acc.astype(sendb.dtype)
+            partial_copy(p).start()
+
+        @pl.when(p >= 2)
+        def _():
+            part[p - 2] = acc
+
+    def spot(z_, y_, c_, x_):
+        return piece.at[x_, pl.ds(2 * ((z_ * 2 + y_) * 2 + c_), 2)]
+
+    lane = lax.broadcasted_iota(jnp.int32, (rank // 2, 2 * rank), 1)
+    for e in range(2):
+        partial_copy(e).wait_recv()
+        low = (part[e] + recvb[e].astype(jnp.float32)).astype(jnp.bfloat16)
+        tmp[e] = lax.dot_general(
+            low, low, (((0,), (0,)), ((), ())), preferred_element_type=jnp.float32
+        )
+        even = tmp[e, pl.ds(0, rank // 2, stride=2), :]
+        odd = tmp[e, pl.ds(1, rank // 2, stride=2), :]
+        flat = jnp.where(lane < rank, pltpu.roll(even, rank, 1), odd) * scale
+        piece[x, 2 * dp + e] = flat.astype(piece.dtype)
+
+    sent = []
+
+    def send(owner, to, s_sem, r_sem):
+        copy = pltpu.make_async_remote_copy(
+            spot(*owner), spot(*owner), s_sem, r_sem, device_id=where_is(*to), device_id_type=MESH
+        )
+        copy.start()
+        sent.append(copy)
+        return copy
+
+    rows = rank // 2
+
+    def widen(owner):
+        z_, y_, c_, x_ = owner
+        first_row = pl.multiple_of(2 * ((z_ * 2 + y_) * 2 + c_) * rows, 2 * rows)
+        wide[x_, pl.ds(first_row, 2 * rows), :] = (
+            spot(*owner)[...].astype(jnp.float32).reshape(2 * rows, 2 * rank)
+        )
+
+    from_z, from_plane, from_core = {}, {}, []
+    order = (0, 1, 3, 2)
+    for j in (2, 1, 3):
+        from_z[j] = send((z, y, c, x), ((z + j) % NZ, y, c, x), zs.at[j - 1], zr.at[j - 1])
+    for k in order:
+        zk = (z + NZ - k) % NZ
+        if k:
+            from_z[k].wait_recv()
+        for d, (dx, dy) in enumerate(PLANE):
+            from_plane[d, k] = send(
+                (zk, y, c, x), (z, flip(y, dy), c, flip(x, dx)), ps.at[d, k], pr.at[d, k]
+            )
+        from_core.append(send((zk, y, c, x), (z, y, 1 - c, x), cs.at[3, k], cr.at[3, k]))
+        widen((zk, y, c, x))
+    for k in order:
+        zk = (z + NZ - k) % NZ
+        for d, (dx, dy) in enumerate(PLANE):
+            from_plane[d, k].wait_recv()
+            owner = (zk, flip(y, dy), c, flip(x, dx))
+            from_core.append(send(owner, (z, y, 1 - c, x), cs.at[d, k], cr.at[d, k]))
+            widen(owner)
+    at = 0
+    for k in order:
+        from_core[at].wait_recv()
+        at += 1
+        widen(((z + NZ - k) % NZ, y, 1 - c, x))
+    for k in order:
+        for dx, dy in PLANE:
+            from_core[at].wait_recv()
+            at += 1
+            widen(((z + NZ - k) % NZ, flip(y, dy), 1 - c, flip(x, dx)))
+
+    examples = scores_o.shape[0]
+    for ck in range(2):
+        for kt in range(rows):
+            q[ck, :, kt * 2 * rank : (kt + 1) * 2 * rank] = wide[
+                ck, pl.ds(kt, examples, stride=rows), :
+            ].astype(q.dtype)
+    get_store.wait()
+    scores = rate[0] * nt_dot(q[0], sbuf[0]) + rate[1] * nt_dot(q[1], sbuf[1])
+    scores_o[...] = scores
+    member = (
+        lax.broadcasted_iota(jnp.int32, (GROUPS, scores.shape[1]), 0) == group[...]
+    ).astype(jnp.float32)
+    mine = z * 0 + (x * 2 + y) * 2 + c
+    t1[mine, :, 0:examples] = nt_dot(member, scores, precision=lax.Precision.HIGHEST)
+    round1 = []
+    for j, (dx, dy, dc) in enumerate(CUBE):
+        copy = pltpu.make_async_remote_copy(
+            t1.at[mine], t1.at[mine], as_.at[j], ar.at[j],
+            device_id=where_is(z, flip(y, dy), flip(c, dc), flip(x, dx)), device_id_type=MESH,
+        )
+        copy.start()
+        round1.append(copy)
+    for copy in round1:
+        copy.wait_recv()
+    total = t1[0]
+    for j in range(1, 8):
+        total += t1[j]
+    t2[z] = total
+    round2 = []
+    for j in (2, 1, 3):
+        copy = pltpu.make_async_remote_copy(
+            t2.at[z], t2.at[z], bs.at[j - 1], br.at[j - 1],
+            device_id=where_is((z + j) % NZ, y, c, x), device_id_type=MESH,
+        )
+        copy.start()
+        round2.append(copy)
+    for copy in round2:
+        copy.wait_recv()
+    total = t2[0]
+    for j in range(1, NZ):
+        total += t2[j]
+    group_o[...] = total[:, 0:examples] * norm
+    for p in range(2):
+        partial_copy(p).wait_send()
+    for copy in sent + round1 + round2:
+        copy.wait_send()
+
+
+def fused(activations, out_grads, proj_in, proj_out, store, ckpt_rate, store_group):
+    ckpts, ex_local, seq_len, ff = activations.shape
+    width = out_grads.shape[3]
+    rank = proj_in.shape[1]
+    devices = lax.axis_size("dp") * lax.axis_size("mp")
+    examples = ex_local * lax.axis_size("dp")
+    rows, depth = store.shape[1:]
+    norm = (GROUPS / (rows * devices)) ** 0.5
+    scale = seq_len ** -0.5
+    hbm = pl.BlockSpec(memory_space=pltpu.HBM)
+    vmem = pl.BlockSpec(memory_space=pltpu.VMEM)
+    bf16, f32 = jnp.bfloat16, jnp.float32
+    dma = pltpu.SemaphoreType.DMA
+    scores, totals = pl.pallas_call(
+        functools.partial(kernel, norm, scale),
+        out_shape=(
+            jax.ShapeDtypeStruct((examples, rows), f32),
+            jax.ShapeDtypeStruct((GROUPS, examples), f32),
+        ),
+        in_specs=[hbm] * 5 + [pl.BlockSpec(memory_space=pltpu.SMEM), vmem],
+        out_specs=(vmem, vmem),
+        scratch_shapes=[
+            pltpu.VMEM((4, seq_len, ff), bf16),
+            pltpu.VMEM((4, seq_len, width), bf16),
+            pltpu.VMEM((2 * rank, ff), bf16),
+            pltpu.VMEM((2 * rank, width), bf16),
+            pltpu.VMEM((ckpts, rows, depth), bf16),
+            pltpu.VMEM((2, seq_len, 2 * rank), f32),
+            pltpu.VMEM((2, seq_len, 2 * rank), bf16),
+            pltpu.VMEM((2, seq_len, 2 * rank), bf16),
+            pltpu.VMEM((ckpts, examples, rank // 2, 2 * rank), bf16),
+            pltpu.VMEM((ckpts, examples * rank // 2, 2 * rank), f32),
+            pltpu.VMEM((ckpts, examples, depth), bf16),
+            pltpu.VMEM((2, 2 * rank, 2 * rank), f32),
+            pltpu.VMEM((8, GROUPS, 128), f32),
+            pltpu.VMEM((NZ, GROUPS, 128), f32),
+            dma((4, 1 + HALVES)), dma((2,)), dma(()),
+            dma((2,)), dma((2,)),
+            dma((3,)), dma((3,)),
+            dma((3, 4)), dma((3, 4)),
+            dma((4, 4)), dma((4, 4)),
+            dma((7,)), dma((7,)),
+            dma((3,)), dma((3,)),
+        ],
+        compiler_params=pltpu.CompilerParams(
+            collective_id=0, has_side_effects=True, vmem_limit_bytes=58 * 2**20
+        ),
+    )(
+        activations, out_grads, proj_in.T, proj_out.T, store, ckpt_rate,
+        store_group.reshape(1, rows),
+    )
+    return scores, totals.T
 
 
 def shards(activations, out_grads, proj_in, proj_out, store, ckpt_rate, store_group):
@@ -19,9 +292,9 @@
     low_grad = summed[..., rank:].astype(jnp.bfloat16)
     outer = jnp.einsum("cesa,cesb->ecab", low_in, low_grad, preferred_element_type=jnp.float32)
     query = (outer.reshape(ex_local, 2, rank * rank) * scale).astype(jnp.bfloat16)
-    piece = lax.all_gather(query, "dp", axis=0, tiled=True)
-    first = jnp.einsum("qk,rk->qr", piece[:, 0], store[0], preferred_element_type=jnp.float32)
-    second = jnp.einsum("qk,rk->qr", piece[:, 1], store[1], preferred_element_type=jnp.float32)
+    gathered = lax.all_gather(query, "dp", axis=0, tiled=True)
+    first = jnp.einsum("qk,rk->qr", gathered[:, 0], store[0], preferred_element_type=jnp.float32)
+    second = jnp.einsum("qk,rk->qr", gathered[:, 1], store[1], preferred_element_type=jnp.float32)
     scores = ckpt_rate[0] * first + ckpt_rate[1] * second
     member = (store_group[:, None] == jnp.arange(GROUPS, dtype=jnp.int32)[None, :]).astype(
         jnp.float32
@@ -43,6 +316,8 @@
         P(),
         P(("dp", "mp")),
     )
+    small = mesh.shape["dp"] == 4 * NZ and mesh.shape["mp"] == 2
     return jax.shard_map(
-        shards, mesh=mesh, in_specs=placed, out_specs=(P(None, ("dp", "mp")), P()), check_vma=False
-    )
+        fused if small else shards,
+        mesh=mesh, in_specs=placed, out_specs=(P(None, ("dp", "mp")), P()), check_vma=False,
+    )

time: 109 us -> 43.6 us (0.40)
  blocking collectives: 84.8 us -> 0 us
  Pallas kernels: 0 us -> 40.1 us
  matrix products: 18.3 us -> 0 us
    psum x2 -> x0, blocking collectives: 61.4 us -> none  [the longest x1 36.9 us: shards(): totals = lax.psum(partial_totals, ('dp', 'mp'))]
    pallas_call x0 -> x1, Pallas kernels: none -> 40.1 us  [fused(): pl.pallas_call(functools.partial(kernel, norm, scale), out_shape=(jax.Sha...]
    all_gather x1 -> x0, blocking collectives: 23.4 us -> none  [shards(): piece = lax.all_gather(query, 'dp', axis=0, tiled=True)]
    dot_general x6 -> x0, matrix products: 18.3 us -> none  [the longest x1 11.5 us: shards(): jnp.einsum('cesf,fr->cesr', activations, proj_in, preferred_element_type=...]
    slice x3 -> x0, local copies, waits for them, and re-layouts: 1.81 us -> none  [the longest x1 1.19 us: shards(): piece[:, 0]]
    unnamed x14 -> x2, local copies, waits for them, and re-layouts: 1.19 us -> 2.67 us
where the time goes in v1:
time: 43.6 us; the launch traced here: 43.4 us
  Pallas kernels  40.1 us (92%)
  local copies, waits for them, and re-layouts  2.67 us (6%)
  between operations  0.64 us (1%)
    pallas_call x1, Pallas kernels, fused(): pl.pallas_call(functools.partial(kernel, norm, scale), out_shape=(jax.Sha...  40.1 us
    unnamed x2, local copies, waits for them, and re-layouts  2.67 us

profile of v1, /device:TPU:0, one launch (start us, length us, event | category | flops | bytes accessed | tf_op | source)
XLA Modules:
  0.0 43.4 jit_solution(17282182898482112044)
XLA Ops:
  0.6 40.1 %shard_map.86 = (f32[32,256]{1,0:T(8,128)}, f32[16,32]{1,0:T(8,128)}) custom-call(bf16[2,2,384,7168]{3,2,1,0:T(8,128)(2,1)} %act.1, bf16[2,2,384,2048]{3,2,1,0:T(8,128)(2,1)} %grad.1, bf16[64,7168]{1,0:T(8,128)(2,1)} %bitcast.4, bf16[64,2048]{1,0:T(8,128)(2,1)} %bitcast.5, bf16[2,256,4096]{2,1,0:T(8,128)(2,1)} %store.1, f32[2]{0:T(128)} %rate.1, ...), custom_call_target="tpu_custom_call" | custom-call | tf_op jit(solution)/shard_map/pallas_call | solution.py:241
  40.7 1.4 %copy.11 = f32[32,256]{1,0:T(8,128)} copy(f32[32,256]{1,0:T(8,128)} %get-tuple-element.8) | data formatting | bytes 65536
  42.1 1.3 %copy.12 = f32[32,16]{0,1:T(8,128)} copy(f32[32,16]{0,1:T(8,128)} %bitcast.6) | data formatting | bytes 4096

commit v2 on v1

--- a/solution.py
+++ b/solution.py
@@ -9,7 +9,7 @@
 GROUPS = 16
 MESH = pl.DeviceIdType.MESH
 NZ = 4
-HALVES = 2
+CUTS = 4
 CUBE = ((1, 0, 0), (0, 1, 0), (1, 1, 0), (0, 0, 1), (1, 0, 1), (0, 1, 1), (1, 1, 1))
 PLANE = ((1, 0), (0, 1), (1, 1))
 
@@ -24,8 +24,8 @@
     norm, scale,
     act, grad, pin, pout, store, rate, group,
     scores_o, group_o,
-    abuf, gbuf, wi, wo, sbuf, part, sendb, recvb, piece, wide, q, tmp, t1, t2,
-    load_sem, w_sem, store_sem, xs, xr, zs, zr, ps, pr, cs, cr, as_, ar, bs, br,
+    abuf, gbuf, wi, wo, sbuf, part, sendb, recvb, qsend, qrecv, piece, wide, q, tmp, t1, t2,
+    load_sem, w_sem, store_sem, xs, xr, qs, qr, zs, zr, ps, pr, cs, cr, as_, ar, bs, br,
 ):
     dp = lax.axis_index("dp")
     x = lax.axis_index("mp")
@@ -34,7 +34,7 @@
     c = dp % 2
     rank = pin.shape[0]
     ff = act.shape[3]
-    cols = ff // HALVES
+    cols = ff // CUTS
 
     def flip(v, on):
         return 1 - v if on else v
@@ -42,29 +42,25 @@
     def where_is(z_, y_, c_, x_):
         return ((z_ * 2 + y_) * 2 + c_, x_)
 
-    def loads(p):
-        ck = (1 - x) + (p // 2) * (2 * x - 1)
-        e = p % 2
-        out = [pltpu.make_async_copy(grad.at[ck, e], gbuf.at[p], load_sem.at[p, 0])]
-        for h in range(HALVES):
-            span = pl.ds(h * cols, cols)
-            out.append(
-                pltpu.make_async_copy(
-                    act.at[ck, e, :, span], abuf.at[p, :, span], load_sem.at[p, 1 + h]
-                )
-            )
-        return out
-
-    w_in = pltpu.make_async_copy(pin, wi.at[pl.ds(0, rank)], w_sem.at[0])
-    w_out = pltpu.make_async_copy(pout, wo.at[pl.ds(rank, rank)], w_sem.at[1])
+    def load(p, h):
+        ck = (1 - x) + p * (2 * x - 1)
+        if h == 0:
+            return pltpu.make_async_copy(grad.at[ck], gbuf.at[p], load_sem.at[p, 0])
+        span = pl.ds((h - 1) * cols, cols)
+        return pltpu.make_async_copy(
+            act.at[ck, :, :, span], abuf.at[p, :, :, span], load_sem.at[p, h]
+        )
+
+    w_in = pltpu.make_async_copy(pin, wi, w_sem.at[0])
+    w_out = pltpu.make_async_copy(pout, wo, w_sem.at[1])
     get_store = pltpu.make_async_copy(store, sbuf, store_sem)
 
     w_out.start()
-    first = loads(0)
-    first[0].start()
+    load(0, 0).start()
+    load(1, 0).start()
     w_in.start()
-    for copy in first[1:]:
-        copy.start()
+    for h in range(1, 1 + CUTS):
+        load(0, h).start()
 
     barrier = pltpu.get_barrier_semaphore()
     friends = [where_is((z + j) % NZ, y, c, x) for j in range(1, NZ)]
@@ -72,59 +68,85 @@
     for friend in friends:
         pl.semaphore_signal(barrier, inc=1, device_id=friend, device_id_type=MESH)
 
-    wi[pl.ds(rank, rank), :] = jnp.zeros((rank, ff), wi.dtype)
-    wo[pl.ds(0, rank), :] = jnp.zeros((rank, wo.shape[1]), wo.dtype)
-    pl.semaphore_wait(barrier, len(friends))
+    peer = where_is(z, y, c, 1 - x)
+    seq = act.shape[2]
+
+    def grad_copy(p):
+        ck = (1 - x) + p * (2 * x - 1)
+        return pltpu.make_async_remote_copy(
+            sendb.at[ck], recvb.at[ck], xs.at[ck], xr.at[ck],
+            device_id=peer, device_id_type=MESH,
+        )
+
+    query_copy = pltpu.make_async_remote_copy(
+        qsend, qrecv, qs, qr, device_id=peer, device_id_type=MESH
+    )
+
     w_out.wait()
+    for p in range(2):
+        ck = (1 - x) + p * (2 * x - 1)
+        load(p, 0).wait()
+        low = nt_dot(gbuf[p].reshape(2 * seq, gbuf.shape[3]), wo[...])
+        low = jnp.concatenate([low[:seq], low[seq:]], axis=1)
+        part[ck] = low
+        sendb[ck] = low.astype(sendb.dtype)
+        if p == 0:
+            pl.semaphore_wait(barrier, len(friends))
+        grad_copy(p).start()
     w_in.wait()
-
-    def partial_copy(p):
-        return pltpu.make_async_remote_copy(
-            sendb.at[p], recvb.at[p], xs.at[p], xr.at[p],
-            device_id=where_is(z, y, c, 1 - x), device_id_type=MESH,
-        )
-
-    @pl.loop(0, 4)
+    side = lax.broadcasted_iota(jnp.int32, (rank, 2 * rank), 1)
+
+    @pl.loop(0, 2)
     def _(p):
-        @pl.when(p < 3)
-        def _():
-            for copy in loads(p + 1):
-                copy.start()
-
-        @pl.when(p == 3)
+        acc = jnp.zeros((2 * seq, rank), jnp.float32)
+        for h in range(1, 1 + CUTS):
+            load(p, h).wait()
+
+            @pl.when(p == 0)
+            def _():
+                load(1, h).start()
+
+            span = slice((h - 1) * cols, h * cols)
+            acc += nt_dot(abuf[p, :, :, span].reshape(2 * seq, cols), wi[:, span])
+        acc = jnp.concatenate([acc[:seq], acc[seq:]], axis=1)
+
+        @pl.when(p == 0)
         def _():
             get_store.start()
-
-        here = loads(p)
-        here[0].wait()
-        acc = nt_dot(gbuf[p], wo[...])
-        for h in range(HALVES):
-            here[1 + h].wait()
-            acc += nt_dot(abuf[p, :, h * cols : (h + 1) * cols], wi[:, h * cols : (h + 1) * cols])
-
-        @pl.when(p < 2)
+            for k in range(2):
+                grad_copy(k).wait_recv()
+
+        ck = (1 - x) + p * (2 * x - 1)
+        low = part[ck] + recvb[ck].astype(jnp.float32)
+        outer = lax.dot_general(
+            acc, low, (((0,), (0,)), ((), ())),
+            preferred_element_type=jnp.float32, precision=lax.Precision.HIGHEST,
+        )
+        outer = jnp.where(side < rank, outer[:rank], outer[rank:])
+
+        @pl.when(p == 0)
         def _():
-            sendb[p] = acc.astype(sendb.dtype)
-            partial_copy(p).start()
-
-        @pl.when(p >= 2)
+            qsend[...] = outer
+            query_copy.start()
+
+        @pl.when(p == 1)
         def _():
-            part[p - 2] = acc
+            tmp[...] = outer
 
     def spot(z_, y_, c_, x_):
         return piece.at[x_, pl.ds(2 * ((z_ * 2 + y_) * 2 + c_), 2)]
 
     lane = lax.broadcasted_iota(jnp.int32, (rank // 2, 2 * rank), 1)
+    query_copy.wait_recv()
+    tmp[...] += qrecv[...]
+    even = tmp[pl.ds(0, rank // 2, stride=2), :]
+    odd = tmp[pl.ds(1, rank // 2, stride=2), :]
+    flat = (
+        jnp.where(lane < rank, even, pltpu.roll(odd, rank, 1)),
+        jnp.where(lane < rank, pltpu.roll(even, rank, 1), odd),
+    )
     for e in range(2):
-        partial_copy(e).wait_recv()
-        low = (part[e] + recvb[e].astype(jnp.float32)).astype(jnp.bfloat16)
-        tmp[e] = lax.dot_general(
-            low, low, (((0,), (0,)), ((), ())), preferred_element_type=jnp.float32
-        )
-        even = tmp[e, pl.ds(0, rank // 2, stride=2), :]
-        odd = tmp[e, pl.ds(1, rank // 2, stride=2), :]
-        flat = jnp.where(lane < rank, pltpu.roll(even, rank, 1), odd) * scale
-        piece[x, 2 * dp + e] = flat.astype(piece.dtype)
+        piece[x, 2 * dp + e] = (flat[e] * scale).astype(piece.dtype)
 
     sent = []
 
@@ -220,7 +242,8 @@
         total += t2[j]
     group_o[...] = total[:, 0:examples] * norm
     for p in range(2):
-        partial_copy(p).wait_send()
+        grad_copy(p).wait_send()
+    query_copy.wait_send()
     for copy in sent + round1 + round2:
         copy.wait_send()
 
@@ -247,22 +270,24 @@
         in_specs=[hbm] * 5 + [pl.BlockSpec(memory_space=pltpu.SMEM), vmem],
         out_specs=(vmem, vmem),
         scratch_shapes=[
-            pltpu.VMEM((4, seq_len, ff), bf16),
-            pltpu.VMEM((4, seq_len, width), bf16),
-            pltpu.VMEM((2 * rank, ff), bf16),
-            pltpu.VMEM((2 * rank, width), bf16),
+            pltpu.VMEM((2, 2, seq_len, ff), bf16),
+            pltpu.VMEM((2, 2, seq_len, width), bf16),
+            pltpu.VMEM((rank, ff), bf16),
+            pltpu.VMEM((rank, width), bf16),
             pltpu.VMEM((ckpts, rows, depth), bf16),
             pltpu.VMEM((2, seq_len, 2 * rank), f32),
             pltpu.VMEM((2, seq_len, 2 * rank), bf16),
             pltpu.VMEM((2, seq_len, 2 * rank), bf16),
+            pltpu.VMEM((rank, 2 * rank), f32),
+            pltpu.VMEM((rank, 2 * rank), f32),
             pltpu.VMEM((ckpts, examples, rank // 2, 2 * rank), bf16),
             pltpu.VMEM((ckpts, examples * rank // 2, 2 * rank), f32),
             pltpu.VMEM((ckpts, examples, depth), bf16),
-            pltpu.VMEM((2, 2 * rank, 2 * rank), f32),
+            pltpu.VMEM((rank, 2 * rank), f32),
             pltpu.VMEM((8, GROUPS, 128), f32),
             pltpu.VMEM((NZ, GROUPS, 128), f32),
-            dma((4, 1 + HALVES)), dma((2,)), dma(()),
-            dma((2,)), dma((2,)),
+            dma((2, 1 + CUTS)), dma((2,)), dma(()),
+            dma((2,)), dma((2,)), dma(()), dma(()),
             dma((3,)), dma((3,)),
             dma((3, 4)), dma((3, 4)),
             dma((4, 4)), dma((4, 4)),

time: 43.6 us -> 46.5 us (1.067)
  Pallas kernels: 40.1 us -> 42.9 us
    pallas_call x1, Pallas kernels: 40.1 us -> 42.9 us  [fused(): pl.pallas_call(functools.partial(kernel, norm, scale), out_shape=(jax.Sha...]
where the time goes in v2:
time: 46.5 us; the launch traced here: 46.2 us
  Pallas kernels  42.9 us (92%)
  local copies, waits for them, and re-layouts  2.67 us (6%)
  between operations  0.64 us (1%)
    pallas_call x1, Pallas kernels, fused(): pl.pallas_call(functools.partial(kernel, norm, scale), out_shape=(jax.Sha...  42.9 us
    unnamed x2, local copies, waits for them, and re-layouts  2.67 us

profile of v2, /device:TPU:0, one launch (start us, length us, event | category | flops | bytes accessed | tf_op | source)
XLA Modules:
  0.0 46.2 jit_solution(13388195044817646793)
XLA Ops:
  0.6 42.9 %shard_map.86 = (f32[32,256]{1,0:T(8,128)}, f32[16,32]{1,0:T(8,128)}) custom-call(bf16[2,2,384,7168]{3,2,1,0:T(8,128)(2,1)} %act.1, bf16[2,2,384,2048]{3,2,1,0:T(8,128)(2,1)} %grad.1, bf16[64,7168]{1,0:T(8,128)(2,1)} %bitcast.4, bf16[64,2048]{1,0:T(8,128)(2,1)} %bitcast.5, bf16[2,256,4096]{2,1,0:T(8,128)(2,1)} %store.1, f32[2]{0:T(128)} %rate.1, ...), custom_call_target="tpu_custom_call" | custom-call | tf_op jit(solution)/shard_map/pallas_call | solution.py:264
  43.5 1.4 %copy.11 = f32[32,256]{1,0:T(8,128)} copy(f32[32,256]{1,0:T(8,128)} %get-tuple-element.8) | data formatting | bytes 65536
  44.9 1.3 %copy.12 = f32[32,16]{0,1:T(8,128)} copy(f32[32,16]{0,1:T(8,128)} %bitcast.6) | data formatting | bytes 4096

commit v3 on v1

--- a/solution.py
+++ b/solution.py
@@ -9,6 +9,7 @@
 GROUPS = 16
 MESH = pl.DeviceIdType.MESH
 NZ = 4
+DIRECT = (2,)
 HALVES = 2
 CUBE = ((1, 0, 0), (0, 1, 0), (1, 1, 0), (0, 0, 1), (1, 0, 1), (0, 1, 1), (1, 1, 1))
 PLANE = ((1, 0), (0, 1), (1, 1))
@@ -25,7 +26,7 @@
     act, grad, pin, pout, store, rate, group,
     scores_o, group_o,
     abuf, gbuf, wi, wo, sbuf, part, sendb, recvb, piece, wide, q, tmp, t1, t2,
-    load_sem, w_sem, store_sem, xs, xr, zs, zr, ps, pr, cs, cr, as_, ar, bs, br,
+    load_sem, w_sem, store_sem, xs, xr, zs, zr, cs, cr, as_, ar, bs, br,
 ):
     dp = lax.axis_index("dp")
     x = lax.axis_index("mp")
@@ -74,7 +75,6 @@
 
     wi[pl.ds(rank, rank), :] = jnp.zeros((rank, ff), wi.dtype)
     wo[pl.ds(0, rank), :] = jnp.zeros((rank, wo.shape[1]), wo.dtype)
-    pl.semaphore_wait(barrier, len(friends))
     w_out.wait()
     w_in.wait()
 
@@ -105,6 +105,11 @@
         @pl.when(p < 2)
         def _():
             sendb[p] = acc.astype(sendb.dtype)
+
+            @pl.when(p == 0)
+            def _():
+                pl.semaphore_wait(barrier, len(friends))
+
             partial_copy(p).start()
 
         @pl.when(p >= 2)
@@ -145,7 +150,7 @@
             spot(*owner)[...].astype(jnp.float32).reshape(2 * rows, 2 * rank)
         )
 
-    from_z, from_plane, from_core = {}, {}, []
+    from_z, arriving, onward = {}, [], []
     order = (0, 1, 3, 2)
     for j in (2, 1, 3):
         from_z[j] = send((z, y, c, x), ((z + j) % NZ, y, c, x), zs.at[j - 1], zr.at[j - 1])
@@ -153,29 +158,25 @@
         zk = (z + NZ - k) % NZ
         if k:
             from_z[k].wait_recv()
-        for d, (dx, dy) in enumerate(PLANE):
-            from_plane[d, k] = send(
-                (zk, y, c, x), (z, flip(y, dy), c, flip(x, dx)), ps.at[d, k], pr.at[d, k]
-            )
-        from_core.append(send((zk, y, c, x), (z, y, 1 - c, x), cs.at[3, k], cr.at[3, k]))
+        for j, (dx, dy, dc) in enumerate(CUBE):
+            if dc and (dx or dy) and k not in DIRECT:
+                continue
+            to = (z, flip(y, dy), flip(c, dc), flip(x, dx))
+            copy = send((zk, y, c, x), to, cs.at[j, k], cr.at[j, k])
+            source = (zk, flip(y, dy), flip(c, dc), flip(x, dx))
+            if not dc and k not in DIRECT:
+                onward.append((copy, source, j + 4, k))
+            else:
+                arriving.append((copy, source))
         widen((zk, y, c, x))
-    for k in order:
-        zk = (z + NZ - k) % NZ
-        for d, (dx, dy) in enumerate(PLANE):
-            from_plane[d, k].wait_recv()
-            owner = (zk, flip(y, dy), c, flip(x, dx))
-            from_core.append(send(owner, (z, y, 1 - c, x), cs.at[d, k], cr.at[d, k]))
-            widen(owner)
-    at = 0
-    for k in order:
-        from_core[at].wait_recv()
-        at += 1
-        widen(((z + NZ - k) % NZ, y, 1 - c, x))
-    for k in order:
-        for dx, dy in PLANE:
-            from_core[at].wait_recv()
-            at += 1
-            widen(((z + NZ - k) % NZ, flip(y, dy), 1 - c, flip(x, dx)))
+    for copy, source, j, k in onward:
+        copy.wait_recv()
+        again = send(source, (z, y, 1 - c, x), cs.at[j, k], cr.at[j, k])
+        arriving.append((again, (source[0], source[1], 1 - c, source[3])))
+        widen(source)
+    for copy, source in arriving:
+        copy.wait_recv()
+        widen(source)
 
     examples = scores_o.shape[0]
     for ck in range(2):
@@ -190,7 +191,10 @@
         lax.broadcasted_iota(jnp.int32, (GROUPS, scores.shape[1]), 0) == group[...]
     ).astype(jnp.float32)
     mine = z * 0 + (x * 2 + y) * 2 + c
-    t1[mine, :, 0:examples] = nt_dot(member, scores, precision=lax.Precision.HIGHEST)
+    half = GROUPS // 2
+    own = nt_dot(member, scores, precision=lax.Precision.HIGHEST)
+    t1[mine, :, 0:examples] = own[:half]
+    t1[mine, :, examples : 2 * examples] = own[half:]
     round1 = []
     for j, (dx, dy, dc) in enumerate(CUBE):
         copy = pltpu.make_async_remote_copy(
@@ -218,7 +222,8 @@
     total = t2[0]
     for j in range(1, NZ):
         total += t2[j]
-    group_o[...] = total[:, 0:examples] * norm
+    group_o[:half, :] = total[:, 0:examples] * norm
+    group_o[half:, :] = total[:, examples : 2 * examples] * norm
     for p in range(2):
         partial_copy(p).wait_send()
     for copy in sent + round1 + round2:
@@ -259,13 +264,12 @@
             pltpu.VMEM((ckpts, examples * rank // 2, 2 * rank), f32),
             pltpu.VMEM((ckpts, examples, depth), bf16),
             pltpu.VMEM((2, 2 * rank, 2 * rank), f32),
-            pltpu.VMEM((8, GROUPS, 128), f32),
-            pltpu.VMEM((NZ, GROUPS, 128), f32),
+            pltpu.VMEM((8, GROUPS // 2, 128), f32),
+            pltpu.VMEM((NZ, GROUPS // 2, 128), f32),
             dma((4, 1 + HALVES)), dma((2,)), dma(()),
             dma((2,)), dma((2,)),
             dma((3,)), dma((3,)),
-            dma((3, 4)), dma((3, 4)),
-            dma((4, 4)), dma((4, 4)),
+                        dma((7, 4)), dma((7, 4)),
             dma((7,)), dma((7,)),
             dma((3,)), dma((3,)),
         ],

time: 43.6 us -> 42.7 us (0.979)
  Pallas kernels: 40.1 us -> 39.2 us
    pallas_call x1, Pallas kernels: 40.1 us -> 39.2 us  [fused(): pl.pallas_call(functools.partial(kernel, norm, scale), out_shape=(jax.Sha...]
where the time goes in v3:
time: 42.7 us; the launch traced here: 42.5 us
  Pallas kernels  39.2 us (92%)
  local copies, waits for them, and re-layouts  2.67 us (6%)
  between operations  0.64 us (1%)
    pallas_call x1, Pallas kernels, fused(): pl.pallas_call(functools.partial(kernel, norm, scale), out_shape=(jax.Sha...  39.2 us
    unnamed x2, local copies, waits for them, and re-layouts  2.67 us

profile of v3, /device:TPU:0, one launch (start us, length us, event | category | flops | bytes accessed | tf_op | source)
XLA Modules:
  0.0 42.5 jit_solution(5430540658762397529)
XLA Ops:
  0.6 39.2 %shard_map.86 = (f32[32,256]{1,0:T(8,128)}, f32[16,32]{1,0:T(8,128)}) custom-call(bf16[2,2,384,7168]{3,2,1,0:T(8,128)(2,1)} %act.1, bf16[2,2,384,2048]{3,2,1,0:T(8,128)(2,1)} %grad.1, bf16[64,7168]{1,0:T(8,128)(2,1)} %bitcast.4, bf16[64,2048]{1,0:T(8,128)(2,1)} %bitcast.5, bf16[2,256,4096]{2,1,0:T(8,128)(2,1)} %store.1, f32[2]{0:T(128)} %rate.1, ...), custom_call_target="tpu_custom_call" | custom-call | tf_op jit(solution)/shard_map/pallas_call | solution.py:246
  39.8 1.4 %copy.11 = f32[32,256]{1,0:T(8,128)} copy(f32[32,256]{1,0:T(8,128)} %get-tuple-element.8) | data formatting | bytes 65536
  41.2 1.3 %copy.12 = f32[32,16]{0,1:T(8,128)} copy(f32[32,16]{0,1:T(8,128)} %bitcast.6) | data formatting | bytes 4096

commit v4 on v3

--- a/solution.py
+++ b/solution.py
@@ -9,7 +9,7 @@
 GROUPS = 16
 MESH = pl.DeviceIdType.MESH
 NZ = 4
-DIRECT = (2,)
+DIRECT = (3, 2)
 HALVES = 2
 CUBE = ((1, 0, 0), (0, 1, 0), (1, 1, 0), (0, 0, 1), (1, 0, 1), (0, 1, 1), (1, 1, 1))
 PLANE = ((1, 0), (0, 1), (1, 1))

time: 42.7 us -> 43.1 us (level)
  no operation moved by 1% of the time
where the time goes in v4:
time: 43.1 us; the launch traced here: 42.9 us
  Pallas kernels  39.6 us (92%)
  local copies, waits for them, and re-layouts  2.67 us (6%)
  between operations  0.64 us (1%)
    pallas_call x1, Pallas kernels, fused(): pl.pallas_call(functools.partial(kernel, norm, scale), out_shape=(jax.Sha...  39.6 us
    unnamed x2, local copies, waits for them, and re-layouts  2.67 us

profile of v4, /device:TPU:0, one launch (start us, length us, event | category | flops | bytes accessed | tf_op | source)
XLA Modules:
  0.0 42.9 jit_solution(9728732810663752883)
XLA Ops:
  0.6 39.6 %shard_map.86 = (f32[32,256]{1,0:T(8,128)}, f32[16,32]{1,0:T(8,128)}) custom-call(bf16[2,2,384,7168]{3,2,1,0:T(8,128)(2,1)} %act.1, bf16[2,2,384,2048]{3,2,1,0:T(8,128)(2,1)} %grad.1, bf16[64,7168]{1,0:T(8,128)(2,1)} %bitcast.4, bf16[64,2048]{1,0:T(8,128)(2,1)} %bitcast.5, bf16[2,256,4096]{2,1,0:T(8,128)(2,1)} %store.1, f32[2]{0:T(128)} %rate.1, ...), custom_call_target="tpu_custom_call" | custom-call | tf_op jit(solution)/shard_map/pallas_call | solution.py:246
  40.2 1.4 %copy.11 = f32[32,256]{1,0:T(8,128)} copy(f32[32,256]{1,0:T(8,128)} %get-tuple-element.8) | data formatting | bytes 65536
  41.6 1.3 %copy.12 = f32[32,16]{0,1:T(8,128)} copy(f32[32,16]{0,1:T(8,128)} %bitcast.6) | data formatting | bytes 4096
